TPU v7x, 512 devices: a whole 4x4x16 slice. The times are simulated.
512 devices in a mesh: dp: 128 (over x, z, core), split: 4 (over y).
Axes of the slice: x: 4, y: 4, z: 16, core: 2. Of those that a mesh axis runs over, the one named last changes fastest.
Arguments:
- embeddings: bfloat16 [131072, 768], P(('dp', 'split')), may hold values from -100 to 100
- cluster_ids: int32 [131072, 1], P(('dp', 'split')), may hold values from 0 to 255; in each aligned block of 256 rows (0 to 255, 256 to 511, ...) at most 4 rows name the same one
- order_ranks: int32 [131072], P(('dp', 'split')), may hold values from 0 to 131071, each once
Outputs:
- nearest: float32 [131072], P(('dp', 'split'))
Inputs may be any that keep to these rules, and one draw needn't show every extreme that they name: `cluster_ids`: among the 256 rows of one device (aligned blocks in order) no cluster is named more than 4 times, a bound that some block reaches; every cluster is named by some row. `order_ranks`: each rank appears once.
All inputs are finite; a program needn't handle non-finite values.
Results may differ from a plain program's by a relative error of at most 0.00056.
Values may be sent and summed in bfloat16 or wider, within the bound.
A program may use at most 64 MiB of HBM per device.

v0:
```python
from functools import partial
import math

import jax
import jax.numpy as jnp
from jax import lax
from jax.sharding import PartitionSpec as P

CLUSTERS = 256
MOST = 4


tile_rows = 512


def unit_rows(embeddings):
    values = embeddings.astype(jnp.float32)
    factor = lax.rsqrt(jnp.mean(values * values, axis=-1, keepdims=True) + 1e-06) * (
        1.0 / math.sqrt(values.shape[-1])
    )
    return (values * factor).astype(jnp.bfloat16)


def pair_tile(queries, query_cluster, query_rank, key_rows, key_cluster, key_rank, want_column):
    scores = lax.dot_general(
        queries, key_rows, (((1,), (1,)), ((), ())), preferred_element_type=jnp.float32
    )
    same = (query_cluster[:, None] == key_cluster[None, :]) & (query_cluster[:, None] >= 0)
    row_mask = same & (key_rank[None, :] < query_rank[:, None])
    row_best = jnp.max(jnp.where(row_mask, scores, -1.0), axis=1)
    column_best = jnp.full((key_rows.shape[0],), -1.0, jnp.float32)
    return (row_best, column_best)


def block_best(queries, query_cluster, query_rank, key_rows, key_cluster, key_rank):
    query_total = queries.shape[0]
    key_total = key_rows.shape[0]
    key_starts = list(range(0, key_total, tile_rows))
    column_parts = [
        jnp.full((min(tile_rows, key_total - begin),), -1.0, jnp.float32) for begin in key_starts
    ]
    row_parts = []
    for query_begin in range(0, query_total, tile_rows):
        query_size = min(tile_rows, query_total - query_begin)
        tile_queries = queries[query_begin : query_begin + query_size]
        tile_qcluster = query_cluster[query_begin : query_begin + query_size]
        tile_qrank = query_rank[query_begin : query_begin + query_size]
        row_acc = jnp.full((query_size,), -1.0, jnp.float32)
        for position, key_begin in enumerate(key_starts):
            key_size = min(tile_rows, key_total - key_begin)
            tile_keys = key_rows[key_begin : key_begin + key_size]
            tile_kcluster = key_cluster[key_begin : key_begin + key_size]
            tile_krank = key_rank[key_begin : key_begin + key_size]
            compute = partial(
                pair_tile,
                tile_queries,
                tile_qcluster,
                tile_qrank,
                tile_keys,
                tile_kcluster,
                tile_krank,
                False,
            )
            row_part, column_part = compute()
            row_acc = jnp.maximum(row_acc, row_part)
        row_parts.append(row_acc)
    return (jnp.concatenate(row_parts), jnp.concatenate(column_parts))


def shards(embeddings, cluster_ids, order_ranks):
    owner_count = lax.axis_size("dp")
    per_owner = CLUSTERS // owner_count
    capacity = per_owner * MOST
    slot_total = owner_count * capacity
    width = embeddings.shape[1]
    unit = unit_rows(embeddings)
    cluster = cluster_ids[:, 0]
    position = jnp.arange(cluster.shape[0], dtype=jnp.int32)
    earlier = (cluster[:, None] == cluster[None, :]) & (position[None, :] < position[:, None])
    place = jnp.sum(earlier.astype(jnp.int32), axis=1)
    target = cluster // per_owner * capacity + cluster % per_owner * MOST + place
    send_rows = jnp.zeros((slot_total, width), jnp.bfloat16).at[target].set(unit)
    send_cluster = jnp.full((slot_total,), -1, jnp.int32).at[target].set(cluster)
    send_rank = jnp.zeros((slot_total,), jnp.int32).at[target].set(order_ranks)
    slot_rows, slot_cluster, slot_rank = (
        lax.all_to_all(send_rows, "dp", split_axis=0, concat_axis=0, tiled=True),
        lax.all_to_all(send_cluster, "dp", split_axis=0, concat_axis=0, tiled=True),
        lax.all_to_all(send_rank, "dp", split_axis=0, concat_axis=0, tiled=True),
    )
    piece_rows = lax.all_gather(slot_rows, "split", axis=0, tiled=True)
    piece_cluster = lax.all_gather(slot_cluster, "split", axis=0, tiled=True)
    piece_rank = lax.all_gather(slot_rank, "split", axis=0, tiled=True)
    row_part, unused = block_best(
        slot_rows, slot_cluster, slot_rank, piece_rows, piece_cluster, piece_rank
    )
    nearest_slot = jnp.maximum(jnp.full((slot_total,), -1.0, jnp.float32), row_part)
    returned = lax.all_to_all(nearest_slot, "dp", split_axis=0, concat_axis=0, tiled=True)
    return returned[target]


def solution(mesh):
    in_specs = (P(("dp", "split"), None), P(("dp", "split"), None), P(("dp", "split")))
    out_specs = P(("dp", "split"))
    return jax.shard_map(shards, mesh=mesh, in_specs=in_specs, out_specs=out_specs, check_vma=False)
```

profile of v0, /device:TPU:1, one launch (start us, length us, event | category | flops | bytes accessed | tf_op | source)
XLA Modules:
  0.0 237.3 jit_solution(6701993411140173319)
XLA Ops:
  6.5 1.2 fusion.16
  7.7 0.9 convert_reduce_fusion
  9.3 2.6 %scatter_custom_fusion.2 = bf16[1024,768]{1,0:T(8,128)(2,1)S(1)} fusion(s32[256]{0:T(256)S(1)} %bitcast.37, bf16[]{:T(256)} %constant.47.clone.1, bf16[256,768]{1,0:T(8,128)(2,1)} %param.3, f32[256]{0:T(256)S(1)} %rsqrt_multiply_fusion), kind=kCustom, calls=%fused_computation.42 | custom fusion | flops 589824 | bytes 1967106 | tf_op jit(solution)/shard_map/scatter | solution.py:82
  12.0 97.1 %all_to_all.45 = bf16[128,8,768]{2,1,0:T(8,128)(2,1)} all-to-all(bf16[128,8,768]{2,1,0:T(8,128)(2,1)S(1)} %bitcast.34), channel_id=1, replica_groups=mesh['dp'=128,'split'=4] {'dp'}, dimensions={0} | all-to-all | bytes 3145728 | tf_op jit(solution)/shard_map/all_to_all | solution.py:86
  109.1 1.7 scatter_custom_fusion.1
  111.5 8.6 %all-to-all-start.1 = ((s32[128,8,1]{1,2,0:T(1,128)}), s32[128,8,1]{1,2,0:T(1,128)S(1)}, u32[]{:S(2)}, u32[]{:S(2)}) async-start(s32[128,8,1]{1,2,0:T(1,128)} %bitcast.4), calls=%async_computation.1 | async-start | bytes 131072 | tf_op jit(solution)/shard_map/all_to_all | solution.py:88
  120.1 1.6 scatter_custom_fusion
  122.3 12.7 %all-to-all-done.1 = s32[128,8,1]{1,2,0:T(1,128)S(1)} async-done(((s32[128,8,1]{1,2,0:T(1,128)}), s32[128,8,1]{1,2,0:T(1,128)S(1)}, u32[]{:S(2)}, u32[]{:S(2)}) %all-to-all-start.1) | async-done | bytes 4128 | tf_op jit(solution)/shard_map/all_to_all | solution.py:88
  135.1 6.6 %all-to-all-start = ((s32[128,8,1]{1,2,0:T(1,128)}), s32[128,8,1]{1,2,0:T(1,128)S(1)}, u32[]{:S(2)}, u32[]{:S(2)}) async-start(s32[128,8,1]{1,2,0:T(1,128)} %bitcast.3), calls=%async_computation | async-start | bytes 131072 | tf_op jit(solution)/shard_map/all_to_all | solution.py:87
  142.4 0.8 reduce.25
  143.5 13.3 %all-to-all-done = s32[128,8,1]{1,2,0:T(1,128)S(1)} async-done(((s32[128,8,1]{1,2,0:T(1,128)}), s32[128,8,1]{1,2,0:T(1,128)S(1)}, u32[]{:S(2)}, u32[]{:S(2)}) %all-to-all-start) | async-done | bytes 4128 | tf_op jit(solution)/shard_map/all_to_all | solution.py:87
  156.8 0.8 reduce.26
  158.0 10.5 %all_gather.10 = s32[4096]{0:T(1024)S(1)} all-gather(s32[1024]{0:T(1024)S(1)} %all_to_all.35), channel_id=1, replica_groups=mesh['dp'=128,'split'=4] {'split'}, dimensions={0}, use_global_device_ids=true | all-gather | bytes 20480 | tf_op jit(solution)/shard_map/all_gather | solution.py:92
  168.6 9.7 %all_gather.9 = s32[4096]{0:T(1024)S(1)} all-gather(s32[1024]{0:T(1024)S(1)} %all_to_all.32), channel_id=1, replica_groups=mesh['dp'=128,'split'=4] {'split'}, dimensions={0}, use_global_device_ids=true | all-gather | bytes 20480 | tf_op jit(solution)/shard_map/all_gather | solution.py:91
  178.4 2.0 fusion
  180.4 1.9 fusion.1
  186.9 2.0 fusion.8
  188.9 2.0 fusion.9
  190.9 1.9 fusion.10
  196.8 0.7 copy.16
  197.5 14.6 %all-to-all-start.3 = ((f32[128,8,1]{1,2,0:T(1,128)}), f32[128,8,1]{1,2,0:T(1,128)S(1)}, u32[]{:S(2)}, u32[]{:S(2)}) async-start(f32[128,8,1]{1,2,0:T(1,128)} %copy.16), calls=%async_computation.3 | async-start | bytes 131072 | tf_op jit(solution)/shard_map/all_to_all | solution.py:97
  212.1 15.0 %all-to-all-done.3 = f32[128,8,1]{1,2,0:T(1,128)S(1)} async-done(((f32[128,8,1]{1,2,0:T(1,128)}), f32[128,8,1]{1,2,0:T(1,128)S(1)}, u32[]{:S(2)}, u32[]{:S(2)}) %all-to-all-start.3) | async-done | bytes 4128 | tf_op jit(solution)/shard_map/all_to_all | solution.py:97
  227.6 0.8 reduce.27
  228.5 1.9 gather_fusion
  (50 shorter events, 12.6 us)
Async XLA Ops:
  6.5 171.8 %all-gather.2.cloned.1.call-start = ((), (), s32[]{:S(2)}) async-start(), calls=%async_computation.4 | async-start | bytes 7864320 | tf_op jit(solution)/shard_map/all_gather | solution.py:90
  109.1 69.3 %copy-start = (bf16[128,8,768]{2,1,0:T(8,128)(2,1)S(1)}, bf16[128,8,768]{2,1,0:T(8,128)(2,1)}, u32[]{:S(2)}) copy-start(bf16[128,8,768]{2,1,0:T(8,128)(2,1)} %all_to_all.45) | copy-start | bytes 4718596
  111.5 23.6 %all-to-all-start.1 = ((s32[128,8,1]{1,2,0:T(1,128)}), s32[128,8,1]{1,2,0:T(1,128)S(1)}, u32[]{:S(2)}, u32[]{:S(2)}) async-start(s32[128,8,1]{1,2,0:T(1,128)} %bitcast.4), calls=%async_computation.1 | async-start | bytes 131072 | tf_op jit(solution)/shard_map/all_to_all | solution.py:88
  135.1 21.7 %all-to-all-start = ((s32[128,8,1]{1,2,0:T(1,128)}), s32[128,8,1]{1,2,0:T(1,128)S(1)}, u32[]{:S(2)}, u32[]{:S(2)}) async-start(s32[128,8,1]{1,2,0:T(1,128)} %bitcast.3), calls=%async_computation | async-start | bytes 131072 | tf_op jit(solution)/shard_map/all_to_all | solution.py:87
  178.4 3.9 %copy-start.1 = (bf16[4096,768]{1,0:T(8,128)(2,1)S(1)}, bf16[4096,768]{1,0:T(8,128)(2,1)}, u32[]{:S(2)}) copy-start(bf16[4096,768]{1,0:T(8,128)(2,1)} %all-gather.2.cloned.1.call-done) | copy-start | bytes 18874372
  186.9 5.9 %slice-start = ((s8[6291456]{0:T(1024)(128)(4,1)}), s8[4194304]{0:T(1024)(128)(4,1)S(1)}, s32[]{:S(2)}) async-start(s8[6291456]{0:T(1024)(128)(4,1)} %bitcast.42), calls=%async_computation.5 | async-start | bytes 8388608
  188.9 3.9 %slice-start.1 = ((s8[6291456]{0:T(1024)(128)(4,1)}), s8[2097152]{0:T(1024)(128)(4,1)S(1)}, s32[]{:S(2)}) async-start(s8[6291456]{0:T(1024)(128)(4,1)} %bitcast.42), calls=%async_computation.6 | async-start | bytes 4194304
  197.5 29.6 %all-to-all-start.3 = ((f32[128,8,1]{1,2,0:T(1,128)}), f32[128,8,1]{1,2,0:T(1,128)S(1)}, u32[]{:S(2)}, u32[]{:S(2)}) async-start(f32[128,8,1]{1,2,0:T(1,128)} %copy.16), calls=%async_computation.3 | async-start | bytes 131072 | tf_op jit(solution)/shard_map/all_to_all | solution.py:97
Sparse Core Ops, SparseCore 0:
  109.2 66.9 all-gather.1
where the time goes:
time: 238 us; the launch traced here: 237 us
  blocking collectives  117 us (49%)
  waiting for transfers between devices  41 us (17%)
  starting transfers between devices  29.8 us (13%)
  matrix products  17.8 us (7%)
  between operations  13.7 us (6%)
  local copies, waits for them, and re-layouts  9.65 us (4%)
  other arithmetic  7.98 us (3%)
    all_to_all x1, blocking collectives, shards(): lax.all_to_all(send_rows, 'dp', split_axis=0, concat_axis=0, tiled=True)  97.1 us
    dot_general x16, matrix products, pair_tile(): lax.dot_general(queries, key_rows, (((1,), (1,)), ((), ())), preferred_el...  17.8 us
    all_to_all x1, waiting for transfers between devices, shards(): lax.all_to_all(nearest_slot, 'dp', split_axis=0, concat_axis=0, tiled=True)  15 us
    all_to_all x1, starting transfers between devices, shards(): lax.all_to_all(nearest_slot, 'dp', split_axis=0, concat_axis=0, tiled=True)  14.6 us
    all_to_all x1, waiting for transfers between devices, shards(): lax.all_to_all(send_cluster, 'dp', split_axis=0, concat_axis=0, tiled=True)  13.3 us
    all_to_all x1, waiting for transfers between devices, shards(): lax.all_to_all(send_rank, 'dp', split_axis=0, concat_axis=0, tiled=True)  12.7 us
    all_gather x1, blocking collectives, shards(): piece_rank = lax.all_gather(slot_rank, 'split', axis=0, tiled=True)  10.5 us
    all_gather x1, blocking collectives, shards(): piece_cluster = lax.all_gather(slot_cluster, 'split', axis=0, tiled=True)  9.73 us
  transfers between devices with their start and end apart: 4, of which 3 were waited for; matrix products, arithmetic and copies ran while one was open for 3% of the time, Pallas kernels for 0%

commit v1 on v0

v1 whole, which is shorter than its diff:
```python
from functools import partial
import math

import jax
import jax.numpy as jnp
from jax import lax
from jax.experimental import pallas as pl
from jax.experimental.pallas import tpu as pltpu
from jax.sharding import PartitionSpec as P

CLUSTERS = 256
MOST = 4
MESH = pl.DeviceIdType.MESH

NX, NY, NZ = 4, 4, 16
ROWS = 256
WIDTH = 768
CAP = 32
GROUP = 4
GROUPS = NZ // GROUP
SLOTS = 16
ZG = CAP * GROUP
XG = SLOTS * NX * NY
BIG = 1 << 22
FAR = float(1 << 20)

STEPS = [0]
for _d in range(1, 8):
    STEPS += [_d, NZ - _d]
STEPS.append(8)


def unit_rows(embeddings):
    values = embeddings.astype(jnp.float32)
    factor = lax.rsqrt(jnp.mean(values * values, axis=-1, keepdims=True) + 1e-06) * (
        1.0 / math.sqrt(values.shape[-1])
    )
    return (values * factor).astype(jnp.bfloat16)


def iota(shape, axis):
    return lax.broadcasted_iota(jnp.int32, shape, axis)


def one_hot(row, count):
    return jnp.where(iota((count, row.shape[1]), 0) == row, 1.0, 0.0)


def places(member):
    n = member.shape[1]
    before = jnp.where(iota((n, n), 0) < iota((n, n), 1), 1.0, 0.0).astype(jnp.bfloat16)
    counts = jnp.dot(member.astype(jnp.bfloat16), before, preferred_element_type=jnp.float32)
    return jnp.sum(member * counts, axis=0, keepdims=True).astype(jnp.int32)


def three_rows(a, b, c):
    sub = iota((8, a.shape[1]), 0)
    rows = jnp.where(sub == 0, a, jnp.where(sub == 1, b, jnp.where(sub == 2, c, 0.0)))
    return rows.astype(jnp.bfloat16)


def place_codes(codes, hot):
    parts = three_rows(
        (codes >> 16).astype(jnp.float32),
        ((codes >> 8) & 255).astype(jnp.float32),
        (codes & 255).astype(jnp.float32),
    )
    moved = lax.dot_general(parts, hot, (((1,), (1,)), ((), ())), preferred_element_type=jnp.float32)
    return (moved[0:1] * 65536.0 + moved[1:2] * 256.0 + moved[2:3]).astype(jnp.int32)


def fetch_values(values, hot):
    high = values.astype(jnp.bfloat16).astype(jnp.float32)
    rest = values - high
    middle = rest.astype(jnp.bfloat16).astype(jnp.float32)
    parts = three_rows(high, middle, rest - middle)
    moved = jnp.dot(parts, hot, preferred_element_type=jnp.float32)
    return (moved[0:1] + moved[1:2]) + moved[2:3]


def kernel(
    emb, cluster, rank, out, flag,
    hot1, hot2, zsend, zrecv, xysend, own, other, key_rank,
    zmeta_out, zmeta_in, xymeta_out, xymeta_in, own_meta, other_meta,
    best_out, xyback, zback_out, zback,
    zmeta_sem, zrow_send, zrow_recv, xymeta_sem, xyrow_send, xyrow_recv,
    cmeta_sem, crow_send, crow_recv, xyback_sem, zback_sem,
):
    dp, y = lax.axis_index("dp"), lax.axis_index("split")
    x, z, core = dp // (2 * NZ), (dp // 2) % NZ, dp % 2

    def along_z(step):
        return ((x * NZ + (z + step + NZ) % NZ) * 2 + core, y)

    def in_plane(e, sign):
        there_x = (x + sign * (e // NY) + NX) % NX
        there_y = (y + sign * (e % NY) + NY) % NY
        return ((there_x * NZ + z) * 2 + core, there_y)

    partner = (dp + 1 - 2 * core, y)

    barrier = pltpu.get_barrier_semaphore()
    for i in range(1, NZ):
        pl.semaphore_signal(barrier, inc=1, device_id=along_z(STEPS[i]), device_id_type=MESH)
    for e in range(1, NX * NY):
        pl.semaphore_signal(barrier, inc=1, device_id=in_plane(e, 1), device_id_type=MESH)
    pl.semaphore_signal(barrier, inc=1, device_id=partner, device_id_type=MESH)

    def send(src, dst, send_sem, recv_sem, device):
        pltpu.make_async_remote_copy(
            src_ref=src, dst_ref=dst, send_sem=send_sem, recv_sem=recv_sem, device_id=device, device_id_type=MESH
        ).start()

    def wait(ref, sem):
        pltpu.make_async_copy(ref, ref, sem).wait()

    ids = cluster[...]
    away = ((ids >> 4) - z) & (NZ - 1)
    step = jnp.where(away == 0, 0, jnp.where(away <= 8, 2 * away - 1, 2 * (NZ - away)))
    place = places(one_hot(step, NZ))
    slot = jnp.where(place < CAP, step * CAP + place, -1)
    most = jnp.max(place.astype(jnp.float32), axis=1, keepdims=True)
    codes = (ids & 15) * 131072 + rank[...] + 1
    for g in range(GROUPS):
        hot = one_hot(slot - g * ZG, ZG).astype(jnp.bfloat16)
        hot1[g * ZG : (g + 1) * ZG, :] = hot
        zmeta_out[g] = jnp.where(most >= CAP, BIG, place_codes(codes, hot))
    zmeta_in[0] = zmeta_out[0]

    unit = unit_rows(emb[...])
    pl.semaphore_wait(barrier, NZ - 1 + NX * NY - 1 + 1)
    for i in range(1, NZ):
        send(zmeta_out.at[i // GROUP], zmeta_in.at[i], zmeta_sem.at[0], zmeta_sem.at[1], along_z(STEPS[i]))
    for g in range(GROUPS):
        rows = jnp.dot(hot1[g * ZG : (g + 1) * ZG, :], unit, preferred_element_type=jnp.float32).astype(jnp.bfloat16)
        zsend[g * ZG : (g + 1) * ZG, :] = rows
        if g == 0:
            zrecv[0:CAP, :] = rows[0:CAP]
        for i in range(max(1, g * GROUP), (g + 1) * GROUP):
            at = pl.ds(i * CAP, CAP)
            send(zsend.at[at], zrecv.at[at], zrow_send.at[0], zrow_recv.at[g], along_z(STEPS[i]))

    wait(zmeta_in.at[pl.ds(1, NZ - 1)], zmeta_sem.at[1])
    lane = iota((1, 128), 1)
    sub = iota((8, 128), 0)
    over = jnp.zeros((1, 1), jnp.float32)
    meta = [jnp.zeros((8, 128), jnp.int32), jnp.zeros((8, 128), jnp.int32)]
    for g in range(GROUPS):
        codes = zmeta_in[g * GROUP]
        for q in range(1, GROUP):
            codes = jnp.where(lane // CAP == q, zmeta_in[g * GROUP + q], codes)
        over = jnp.maximum(over, jnp.max(codes.astype(jnp.float32), axis=1, keepdims=True))
        filled = (codes > 0) & (codes < BIG)
        value = codes - 1
        local = value >> 17
        e = (((local >> 2) - x) & 3) * NY + (((local & 3) - y) & 3)
        e = jnp.where(filled, e, NX * NY)
        slot2 = jnp.where(filled, e * SLOTS + places(one_hot(e, NX * NY)), -1)
        hot = one_hot(slot2, XG).astype(jnp.bfloat16)
        hot2[g * XG : (g + 1) * XG, :] = hot
        ranks = place_codes(jnp.where(filled, (value & 131071) + 1, 0), hot)
        for h in range(2):
            meta[h] = jnp.where(sub == g, ranks[:, h * 128 : (h + 1) * 128], meta[h])
    for h in range(2):
        xymeta_out[h] = jnp.where(over >= BIG, BIG, meta[h])
    xymeta_in[0] = xymeta_out[0]
    for e in range(1, NX * NY):
        send(xymeta_out.at[e // 8], xymeta_in.at[e], xymeta_sem.at[0], xymeta_sem.at[1], in_plane(e, 1))
    wait(xymeta_in.at[pl.ds(1, NX * NY - 1)], xymeta_sem.at[1])
    lane8 = iota((8, 128), 1)
    for h in range(2):
        merged = xymeta_in[h * 8]
        for e in range(1, 8):
            merged = jnp.where(lane8 // SLOTS == e, xymeta_in[h * 8 + e], merged)
        own_meta[h] = merged
    send(own_meta, other_meta, cmeta_sem.at[0], cmeta_sem.at[1], partner)
    wait(other_meta, cmeta_sem.at[1])
    top = jnp.zeros((8, 128), jnp.float32)
    query_rank = []
    for which, ref in enumerate((own_meta, other_meta)):
        for h in range(2):
            tile = ref[h]
            top = jnp.maximum(top, tile.astype(jnp.float32))
            for g in range(GROUPS):
                row = tile[g : g + 1].astype(jnp.float32)
                key = jnp.where(row > 0.0, row, FAR)
                at = which * GROUPS * XG + g * XG + h * 128
                key_rank[at : at + 128, :] = jnp.transpose(jnp.broadcast_to(key, (128, 128)))
    flag[...] = jnp.where(jnp.max(top, axis=(0, 1), keepdims=True) >= BIG, 1, 0) + jnp.zeros((8, 128), jnp.int32)
    for g in range(GROUPS):
        query_rank.append(
            jnp.concatenate([own_meta[0][g : g + 1], own_meta[1][g : g + 1]], axis=1).astype(jnp.float32)
        )
    best = [jnp.full((1, XG), -1.0, jnp.float32) for _ in range(GROUPS)]

    def score(which, first, last, g0, g1):
        ref = (own, other)[which]
        scores = lax.dot_general(
            ref[first * XG : last * XG, :],
            own[g0 * XG : g1 * XG, :],
            (((1,), (1,)), ((), ())),
            preferred_element_type=jnp.float32,
        )
        base = which * GROUPS * XG
        ranks = key_rank[base + first * XG : base + last * XG, :]
        for g in range(g0, g1):
            for h in range(2):
                at = (g - g0) * XG + h * 128
                earlier = ranks < query_rank[g][:, h * 128 : (h + 1) * 128]
                part = jnp.max(jnp.where(earlier, scores[:, at : at + 128], -1.0), axis=0, keepdims=True)
                halves[g][h] = jnp.maximum(halves[g][h], part)

    halves = [[row[:, 0:128], row[:, 128:256]] for row in best]

    def score_group(which, g):
        score(which, 0, g + 1, g, g + 1)
        if g:
            score(which, g, g + 1, 0, g)

    def group_in_plane(g):
        first = max(1, g * GROUP)
        wait(zrecv.at[pl.ds(first * CAP, ((g + 1) * GROUP - first) * CAP)], zrow_recv.at[g])
        rows = jnp.dot(
            hot2[g * XG : (g + 1) * XG, :], zrecv[g * ZG : (g + 1) * ZG, :], preferred_element_type=jnp.float32
        ).astype(jnp.bfloat16)
        xysend[g * XG : (g + 1) * XG, :] = rows
        own[g * XG : g * XG + SLOTS, :] = rows[0:SLOTS]
        for e in range(1, NX * NY):
            at = pl.ds(g * XG + e * SLOTS, SLOTS)
            send(xysend.at[at], own.at[at], xyrow_send.at[0], xyrow_recv.at[g], in_plane(e, 1))

    def group_to_partner(g):
        wait(own.at[pl.ds(g * XG + SLOTS, XG - SLOTS)], xyrow_recv.at[g])
        at = pl.ds(g * XG, XG)
        send(own.at[at], other.at[at], crow_send.at[0], crow_recv.at[g], partner)

    def group_from_partner(g):
        wait(other.at[pl.ds(g * XG, XG)], crow_recv.at[g])

    for g in range(GROUPS):
        group_in_plane(g)
        if g >= 1:
            group_to_partner(g - 1)
        if g >= 2:
            group_from_partner(g - 2)
            for which in range(2):
                score_group(which, g - 2)
    group_from_partner(GROUPS - 2)
    for which in range(2):
        score_group(which, GROUPS - 2)
    group_to_partner(GROUPS - 1)
    score_group(0, GROUPS - 1)
    group_from_partner(GROUPS - 1)
    score_group(1, GROUPS - 1)

    for h in range(2):
        tile = jnp.zeros((8, 128), jnp.float32)
        for g in range(GROUPS):
            tile = jnp.where(sub == g, halves[g][h], tile)
        best_out[h] = tile
    xyback[0] = best_out[0]
    for e in range(1, NX * NY):
        send(best_out.at[e // 8], xyback.at[e], xyback_sem.at[0], xyback_sem.at[1], in_plane(e, -1))
    wait(xyback.at[pl.ds(1, NX * NY - 1)], xyback_sem.at[1])
    merged = []
    for h in range(2):
        tile = xyback[h * 8]
        for e in range(1, 8):
            tile = jnp.where(lane8 // SLOTS == e, xyback[h * 8 + e], tile)
        merged.append(tile)
    for g in range(GROUPS):
        row = jnp.concatenate([merged[0][g : g + 1], merged[1][g : g + 1]], axis=1)
        zback_out[g] = fetch_values(row, hot2[g * XG : (g + 1) * XG, :])
    zback[0] = zback_out[0]
    for i in range(1, NZ):
        send(zback_out.at[i // GROUP], zback.at[i], zback_sem.at[0], zback_sem.at[1], along_z(-STEPS[i]))
    wait(zback.at[pl.ds(1, NZ - 1)], zback_sem.at[1])
    parts = []
    for g in range(GROUPS):
        row = zback[g * GROUP]
        for q in range(1, GROUP):
            row = jnp.where(lane // CAP == q, zback[g * GROUP + q], row)
        parts.append(row)
    out[...] = fetch_values(jnp.concatenate(parts, axis=1), hot1[...])

    wait(zmeta_in.at[pl.ds(1, NZ - 1)], zmeta_sem.at[0])
    wait(zsend.at[pl.ds(CAP, (NZ - 1) * CAP)], zrow_send.at[0])
    wait(xymeta_in.at[pl.ds(1, NX * NY - 1)], xymeta_sem.at[0])
    for g in range(GROUPS):
        wait(own.at[pl.ds(g * XG + SLOTS, XG - SLOTS)], xyrow_send.at[0])
    wait(own_meta, cmeta_sem.at[0])
    wait(own, crow_send.at[0])
    wait(xyback.at[pl.ds(1, NX * NY - 1)], xyback_sem.at[0])
    wait(zback.at[pl.ds(1, NZ - 1)], zback_sem.at[0])


def fast(embeddings, cluster_ids, order_ranks):
    vmem = pl.BlockSpec(memory_space=pltpu.VMEM)
    bf16, f32, i32 = jnp.bfloat16, jnp.float32, jnp.int32
    pair = pltpu.SemaphoreType.DMA((2,))
    one = pltpu.SemaphoreType.DMA((1,))
    each = pltpu.SemaphoreType.DMA((GROUPS,))
    return pl.pallas_call(
        kernel,
        out_shape=(jax.ShapeDtypeStruct((1, ROWS), f32), jax.ShapeDtypeStruct((8, 128), i32)),
        in_specs=[vmem] * 3,
        out_specs=(vmem, vmem),
        scratch_shapes=[
            pltpu.VMEM((GROUPS * ZG, ROWS), bf16),
            pltpu.VMEM((GROUPS * XG, ZG), bf16),
            pltpu.VMEM((GROUPS * ZG, WIDTH), bf16),
            pltpu.VMEM((GROUPS * ZG, WIDTH), bf16),
            pltpu.VMEM((GROUPS * XG, WIDTH), bf16),
            pltpu.VMEM((GROUPS * XG, WIDTH), bf16),
            pltpu.VMEM((GROUPS * XG, WIDTH), bf16),
            pltpu.VMEM((2 * GROUPS * XG, 128), f32),
            pltpu.VMEM((GROUPS, 1, 128), i32),
            pltpu.VMEM((NZ, 1, 128), i32),
            pltpu.VMEM((2, 8, 128), i32),
            pltpu.VMEM((NX * NY, 8, 128), i32),
            pltpu.VMEM((2, 8, 128), i32),
            pltpu.VMEM((2, 8, 128), i32),
            pltpu.VMEM((2, 8, 128), f32),
            pltpu.VMEM((NX * NY, 8, 128), f32),
            pltpu.VMEM((GROUPS, 1, 128), f32),
            pltpu.VMEM((NZ, 1, 128), f32),
            pair, one, each, pair, one, each, pair, one, each, pair, pair,
        ],
        compiler_params=pltpu.CompilerParams(
            collective_id=0, has_side_effects=True, vmem_limit_bytes=40 * 1024 * 1024
        ),
    )(embeddings, cluster_ids.reshape(1, ROWS), order_ranks.reshape(1, ROWS))


def pair_tile(queries, query_cluster, query_rank, key_rows, key_cluster, key_rank):
    scores = lax.dot_general(queries, key_rows, (((1,), (1,)), ((), ())), preferred_element_type=jnp.float32)
    same = (query_cluster[:, None] == key_cluster[None, :]) & (query_cluster[:, None] >= 0)
    row_mask = same & (key_rank[None, :] < query_rank[:, None])
    return jnp.max(jnp.where(row_mask, scores, -1.0), axis=1)


def padded(embeddings, cluster_ids, order_ranks):
    owner_count = lax.axis_size("dp")
    per_owner = CLUSTERS // owner_count
    capacity = per_owner * MOST
    slot_total = owner_count * capacity
    unit = unit_rows(embeddings)
    cluster = cluster_ids[:, 0]
    position = jnp.arange(cluster.shape[0], dtype=jnp.int32)
    earlier = (cluster[:, None] == cluster[None, :]) & (position[None, :] < position[:, None])
    place = jnp.sum(earlier.astype(jnp.int32), axis=1)
    target = cluster // per_owner * capacity + cluster % per_owner * MOST + place
    send_rows = jnp.zeros((slot_total, embeddings.shape[1]), jnp.bfloat16).at[target].set(unit)
    send_cluster = jnp.full((slot_total,), -1, jnp.int32).at[target].set(cluster)
    send_rank = jnp.zeros((slot_total,), jnp.int32).at[target].set(order_ranks)
    slots = [
        lax.all_to_all(a, "dp", split_axis=0, concat_axis=0, tiled=True) for a in (send_rows, send_cluster, send_rank)
    ]
    pieces = [lax.all_gather(a, "split", axis=0, tiled=True) for a in slots]
    tile = 512
    parts = []
    for begin in range(0, slot_total, tile):
        mine = [a[begin : begin + tile] for a in slots]
        best = jnp.full((tile,), -1.0, jnp.float32)
        for key in range(0, pieces[0].shape[0], tile):
            best = jnp.maximum(best, pair_tile(*mine, *[a[key : key + tile] for a in pieces]))
        parts.append(best)
    returned = lax.all_to_all(jnp.concatenate(parts), "dp", split_axis=0, concat_axis=0, tiled=True)
    return returned[target]


def shards(embeddings, cluster_ids, order_ranks):
    nearest, flag = fast(embeddings, cluster_ids, order_ranks)
    return lax.cond(
        flag[0, 0] > 0,
        lambda: padded(embeddings, cluster_ids, order_ranks),
        lambda: nearest.reshape(ROWS),
    )


def solution(mesh):
    in_specs = (P(("dp", "split"), None), P(("dp", "split"), None), P(("dp", "split")))
    out_specs = P(("dp", "split"))
    return jax.shard_map(shards, mesh=mesh, in_specs=in_specs, out_specs=out_specs, check_vma=False)
```

time: 238 us -> 93.8 us (0.39)
  blocking collectives: 117 us -> 0 us
  Pallas kernels: 0 us -> 78.4 us
  waiting for transfers between devices: 41 us -> 0 us
  starting transfers between devices: 29.8 us -> 0 us
  matrix products: 17.8 us -> 0 us
  local copies, waits for them, and re-layouts: 9.65 us -> 1.08 us
  other arithmetic: 7.98 us -> 0 us
    all_to_all x1 -> x0, blocking collectives: 97.1 us -> none  [shards(): lax.all_to_all(send_rows, 'dp', split_axis=0, concat_axis=0, tiled=True)]
    pallas_call x0 -> x1, Pallas kernels: none -> 78.4 us  [fast(): pl.pallas_call(kernel, out_shape=(jax.ShapeDtypeStruct((1, ROWS), f32), j...]
    all_to_all x3 -> x0, waiting for transfers between devices: 41 us -> none  [the longest x1 15 us: shards(): lax.all_to_all(nearest_slot, 'dp', split_axis=0, concat_axis=0, tiled=True)]
    all_to_all x3 -> x0, starting transfers between devices: 29.8 us -> none  [the longest x1 14.6 us: shards(): lax.all_to_all(nearest_slot, 'dp', split_axis=0, concat_axis=0, tiled=True)]
    all_gather x2 -> x0, blocking collectives: 20.3 us -> none  [the longest x1 10.5 us: shards(): piece_rank = lax.all_gather(slot_rank, 'split', axis=0, tiled=True)]
    dot_general x16 -> x0, matrix products: 17.8 us -> none  [pair_tile(): lax.dot_general(queries, key_rows, (((1,), (1,)), ((), ())), preferred_el...]
    scatter x2 -> x0, local copies, waits for them, and re-layouts: 3.25 us -> none  [the longest x1 1.69 us: shards(): send_rank = jnp.zeros((slot_total,), jnp.int32).at[target].set(order_ranks)]
    all_to_all x7 -> x0, local copies, waits for them, and re-layouts: 2.7 us -> none  [the longest x3 1.31 us: shards(): lax.all_to_all(send_rank, 'dp', split_axis=0, concat_axis=0, tiled=True)]
  transfers between devices with their start and end apart: 4 -> 0, of which waited for: 3 -> 0; matrix products, arithmetic and copies ran while one was open for 3% -> 0% of each run, Pallas kernels for 0% -> 0%
where the time goes in v1:
time: 93.8 us; the launch traced here: 93.7 us
  Pallas kernels  78.4 us (84%)
  between operations  14 us (15%)
  local copies, waits for them, and re-layouts  1.08 us (1%)
    pallas_call x1, Pallas kernels, fast(): pl.pallas_call(kernel, out_shape=(jax.ShapeDtypeStruct((1, ROWS), f32), j...  78.4 us

profile of v1, /device:TPU:1, one launch (start us, length us, event | category | flops | bytes accessed | tf_op | source)
XLA Modules:
  0.0 93.7 jit_solution(8662316822299022091)
XLA Ops:
  6.5 78.4 %shard_map.39 = (f32[1,256]{1,0:T(1,128)S(1)}, s32[8,128]{1,0:T(8,128)S(1)}) custom-call(bf16[256,768]{1,0:T(8,128)(2,1)} %emb.1, s32[1,256]{1,0:T(1,128)} %bitcast.40, s32[1,256]{1,0:T(1,128)} %bitcast.48), custom_call_target="tpu_custom_call" | custom-call | tf_op jit(solution)/shard_map/pallas_call | solution.py:303
  84.9 0.5 slice.127
  86.1 0.2 conditional.1
  86.3 0.6 copy.17

commit v2 on v1

--- a/solution.py
+++ b/solution.py
@@ -8,18 +8,16 @@
 from jax.experimental.pallas import tpu as pltpu
 from jax.sharding import PartitionSpec as P
 
-CLUSTERS = 256
-MOST = 4
 MESH = pl.DeviceIdType.MESH
 
 NX, NY, NZ = 4, 4, 16
 ROWS = 256
 WIDTH = 768
 CAP = 32
+FULL = 64
 GROUP = 4
 GROUPS = NZ // GROUP
 SLOTS = 16
-ZG = CAP * GROUP
 XG = SLOTS * NX * NY
 BIG = 1 << 22
 FAR = float(1 << 20)
@@ -79,6 +77,7 @@
 
 
 def kernel(
+    cap,
     emb, cluster, rank, out, flag,
     hot1, hot2, zsend, zrecv, xysend, own, other, key_rank,
     zmeta_out, zmeta_in, xymeta_out, xymeta_in, own_meta, other_meta,
@@ -86,6 +85,9 @@
     zmeta_sem, zrow_send, zrow_recv, xymeta_sem, xyrow_send, xyrow_recv,
     cmeta_sem, crow_send, crow_recv, xyback_sem, zback_sem,
 ):
+    zg = cap * GROUP
+    per = 128 // cap
+    tiles = zg // 128
     dp, y = lax.axis_index("dp"), lax.axis_index("split")
     x, z, core = dp // (2 * NZ), (dp // 2) % NZ, dp % 2
 
@@ -118,37 +120,47 @@
     away = ((ids >> 4) - z) & (NZ - 1)
     step = jnp.where(away == 0, 0, jnp.where(away <= 8, 2 * away - 1, 2 * (NZ - away)))
     place = places(one_hot(step, NZ))
-    slot = jnp.where(place < CAP, step * CAP + place, -1)
+    slot = jnp.where(place < cap, step * cap + place, -1)
     most = jnp.max(place.astype(jnp.float32), axis=1, keepdims=True)
     codes = (ids & 15) * 131072 + rank[...] + 1
     for g in range(GROUPS):
-        hot = one_hot(slot - g * ZG, ZG).astype(jnp.bfloat16)
-        hot1[g * ZG : (g + 1) * ZG, :] = hot
-        zmeta_out[g] = jnp.where(most >= CAP, BIG, place_codes(codes, hot))
+        hot = one_hot(slot - g * zg, zg).astype(jnp.bfloat16)
+        hot1[g * zg : (g + 1) * zg, :] = hot
+        placed = jnp.where(most >= cap, BIG, place_codes(codes, hot))
+        for t in range(tiles):
+            zmeta_out[g * tiles + t] = placed[:, t * 128 : (t + 1) * 128]
     zmeta_in[0] = zmeta_out[0]
 
     unit = unit_rows(emb[...])
     pl.semaphore_wait(barrier, NZ - 1 + NX * NY - 1 + 1)
     for i in range(1, NZ):
-        send(zmeta_out.at[i // GROUP], zmeta_in.at[i], zmeta_sem.at[0], zmeta_sem.at[1], along_z(STEPS[i]))
-    for g in range(GROUPS):
-        rows = jnp.dot(hot1[g * ZG : (g + 1) * ZG, :], unit, preferred_element_type=jnp.float32).astype(jnp.bfloat16)
-        zsend[g * ZG : (g + 1) * ZG, :] = rows
+        send(zmeta_out.at[i // per], zmeta_in.at[i], zmeta_sem.at[0], zmeta_sem.at[1], along_z(STEPS[i]))
+    for g in range(GROUPS):
+        rows = jnp.dot(hot1[g * zg : (g + 1) * zg, :], unit, preferred_element_type=jnp.float32).astype(jnp.bfloat16)
+        zsend[g * zg : (g + 1) * zg, :] = rows
         if g == 0:
-            zrecv[0:CAP, :] = rows[0:CAP]
+            zrecv[0:cap, :] = rows[0:cap]
         for i in range(max(1, g * GROUP), (g + 1) * GROUP):
-            at = pl.ds(i * CAP, CAP)
+            at = pl.ds(i * cap, cap)
             send(zsend.at[at], zrecv.at[at], zrow_send.at[0], zrow_recv.at[g], along_z(STEPS[i]))
 
     wait(zmeta_in.at[pl.ds(1, NZ - 1)], zmeta_sem.at[1])
     lane = iota((1, 128), 1)
+
+    def merge(ref, g):
+        rows = []
+        for first in range(g * GROUP, (g + 1) * GROUP, per):
+            row = ref[first]
+            for q in range(1, per):
+                row = jnp.where(lane // cap == q, ref[first + q], row)
+            rows.append(row)
+        return rows[0] if tiles == 1 else jnp.concatenate(rows, axis=1)
+
     sub = iota((8, 128), 0)
     over = jnp.zeros((1, 1), jnp.float32)
     meta = [jnp.zeros((8, 128), jnp.int32), jnp.zeros((8, 128), jnp.int32)]
     for g in range(GROUPS):
-        codes = zmeta_in[g * GROUP]
-        for q in range(1, GROUP):
-            codes = jnp.where(lane // CAP == q, zmeta_in[g * GROUP + q], codes)
+        codes = merge(zmeta_in, g)
         over = jnp.maximum(over, jnp.max(codes.astype(jnp.float32), axis=1, keepdims=True))
         filled = (codes > 0) & (codes < BIG)
         value = codes - 1
@@ -186,7 +198,7 @@
                 key = jnp.where(row > 0.0, row, FAR)
                 at = which * GROUPS * XG + g * XG + h * 128
                 key_rank[at : at + 128, :] = jnp.transpose(jnp.broadcast_to(key, (128, 128)))
-    flag[...] = jnp.where(jnp.max(top, axis=(0, 1), keepdims=True) >= BIG, 1, 0) + jnp.zeros((8, 128), jnp.int32)
+    flag[...] = jnp.where(jnp.max(top, axis=(0, 1), keepdims=True) >= BIG, 1, 0)
     for g in range(GROUPS):
         query_rank.append(
             jnp.concatenate([own_meta[0][g : g + 1], own_meta[1][g : g + 1]], axis=1).astype(jnp.float32)
@@ -219,9 +231,9 @@
 
     def group_in_plane(g):
         first = max(1, g * GROUP)
-        wait(zrecv.at[pl.ds(first * CAP, ((g + 1) * GROUP - first) * CAP)], zrow_recv.at[g])
+        wait(zrecv.at[pl.ds(first * cap, ((g + 1) * GROUP - first) * cap)], zrow_recv.at[g])
         rows = jnp.dot(
-            hot2[g * XG : (g + 1) * XG, :], zrecv[g * ZG : (g + 1) * ZG, :], preferred_element_type=jnp.float32
+            hot2[g * XG : (g + 1) * XG, :], zrecv[g * zg : (g + 1) * zg, :], preferred_element_type=jnp.float32
         ).astype(jnp.bfloat16)
         xysend[g * XG : (g + 1) * XG, :] = rows
         own[g * XG : g * XG + SLOTS, :] = rows[0:SLOTS]
@@ -270,21 +282,17 @@
         merged.append(tile)
     for g in range(GROUPS):
         row = jnp.concatenate([merged[0][g : g + 1], merged[1][g : g + 1]], axis=1)
-        zback_out[g] = fetch_values(row, hot2[g * XG : (g + 1) * XG, :])
+        fetched = fetch_values(row, hot2[g * XG : (g + 1) * XG, :])
+        for t in range(tiles):
+            zback_out[g * tiles + t] = fetched[:, t * 128 : (t + 1) * 128]
     zback[0] = zback_out[0]
     for i in range(1, NZ):
-        send(zback_out.at[i // GROUP], zback.at[i], zback_sem.at[0], zback_sem.at[1], along_z(-STEPS[i]))
+        send(zback_out.at[i // per], zback.at[i], zback_sem.at[0], zback_sem.at[1], along_z(-STEPS[i]))
     wait(zback.at[pl.ds(1, NZ - 1)], zback_sem.at[1])
-    parts = []
-    for g in range(GROUPS):
-        row = zback[g * GROUP]
-        for q in range(1, GROUP):
-            row = jnp.where(lane // CAP == q, zback[g * GROUP + q], row)
-        parts.append(row)
-    out[...] = fetch_values(jnp.concatenate(parts, axis=1), hot1[...])
+    out[...] = fetch_values(jnp.concatenate([merge(zback, g) for g in range(GROUPS)], axis=1), hot1[...])
 
     wait(zmeta_in.at[pl.ds(1, NZ - 1)], zmeta_sem.at[0])
-    wait(zsend.at[pl.ds(CAP, (NZ - 1) * CAP)], zrow_send.at[0])
+    wait(zsend.at[pl.ds(cap, (NZ - 1) * cap)], zrow_send.at[0])
     wait(xymeta_in.at[pl.ds(1, NX * NY - 1)], xymeta_sem.at[0])
     for g in range(GROUPS):
         wait(own.at[pl.ds(g * XG + SLOTS, XG - SLOTS)], xyrow_send.at[0])
@@ -294,27 +302,27 @@
     wait(zback.at[pl.ds(1, NZ - 1)], zback_sem.at[0])
 
 
-def fast(embeddings, cluster_ids, order_ranks):
+def exchange(cap, collective_id, embeddings, cluster_ids, order_ranks):
     vmem = pl.BlockSpec(memory_space=pltpu.VMEM)
     bf16, f32, i32 = jnp.bfloat16, jnp.float32, jnp.int32
     pair = pltpu.SemaphoreType.DMA((2,))
     one = pltpu.SemaphoreType.DMA((1,))
     each = pltpu.SemaphoreType.DMA((GROUPS,))
     return pl.pallas_call(
-        kernel,
-        out_shape=(jax.ShapeDtypeStruct((1, ROWS), f32), jax.ShapeDtypeStruct((8, 128), i32)),
+        partial(kernel, cap),
+        out_shape=(jax.ShapeDtypeStruct((1, ROWS), f32), jax.ShapeDtypeStruct((1, 1), i32)),
         in_specs=[vmem] * 3,
         out_specs=(vmem, vmem),
         scratch_shapes=[
-            pltpu.VMEM((GROUPS * ZG, ROWS), bf16),
-            pltpu.VMEM((GROUPS * XG, ZG), bf16),
-            pltpu.VMEM((GROUPS * ZG, WIDTH), bf16),
-            pltpu.VMEM((GROUPS * ZG, WIDTH), bf16),
+            pltpu.VMEM((NZ * cap, ROWS), bf16),
+            pltpu.VMEM((GROUPS * XG, GROUP * cap), bf16),
+            pltpu.VMEM((NZ * cap, WIDTH), bf16),
+            pltpu.VMEM((NZ * cap, WIDTH), bf16),
             pltpu.VMEM((GROUPS * XG, WIDTH), bf16),
             pltpu.VMEM((GROUPS * XG, WIDTH), bf16),
             pltpu.VMEM((GROUPS * XG, WIDTH), bf16),
             pltpu.VMEM((2 * GROUPS * XG, 128), f32),
-            pltpu.VMEM((GROUPS, 1, 128), i32),
+            pltpu.VMEM((NZ * cap // 128, 1, 128), i32),
             pltpu.VMEM((NZ, 1, 128), i32),
             pltpu.VMEM((2, 8, 128), i32),
             pltpu.VMEM((NX * NY, 8, 128), i32),
@@ -322,60 +330,21 @@
             pltpu.VMEM((2, 8, 128), i32),
             pltpu.VMEM((2, 8, 128), f32),
             pltpu.VMEM((NX * NY, 8, 128), f32),
-            pltpu.VMEM((GROUPS, 1, 128), f32),
+            pltpu.VMEM((NZ * cap // 128, 1, 128), f32),
             pltpu.VMEM((NZ, 1, 128), f32),
             pair, one, each, pair, one, each, pair, one, each, pair, pair,
         ],
         compiler_params=pltpu.CompilerParams(
-            collective_id=0, has_side_effects=True, vmem_limit_bytes=40 * 1024 * 1024
+            collective_id=collective_id, has_side_effects=True, vmem_limit_bytes=40 * 1024 * 1024
         ),
-    )(embeddings, cluster_ids.reshape(1, ROWS), order_ranks.reshape(1, ROWS))
-
-
-def pair_tile(queries, query_cluster, query_rank, key_rows, key_cluster, key_rank):
-    scores = lax.dot_general(queries, key_rows, (((1,), (1,)), ((), ())), preferred_element_type=jnp.float32)
-    same = (query_cluster[:, None] == key_cluster[None, :]) & (query_cluster[:, None] >= 0)
-    row_mask = same & (key_rank[None, :] < query_rank[:, None])
-    return jnp.max(jnp.where(row_mask, scores, -1.0), axis=1)
-
-
-def padded(embeddings, cluster_ids, order_ranks):
-    owner_count = lax.axis_size("dp")
-    per_owner = CLUSTERS // owner_count
-    capacity = per_owner * MOST
-    slot_total = owner_count * capacity
-    unit = unit_rows(embeddings)
-    cluster = cluster_ids[:, 0]
-    position = jnp.arange(cluster.shape[0], dtype=jnp.int32)
-    earlier = (cluster[:, None] == cluster[None, :]) & (position[None, :] < position[:, None])
-    place = jnp.sum(earlier.astype(jnp.int32), axis=1)
-    target = cluster // per_owner * capacity + cluster % per_owner * MOST + place
-    send_rows = jnp.zeros((slot_total, embeddings.shape[1]), jnp.bfloat16).at[target].set(unit)
-    send_cluster = jnp.full((slot_total,), -1, jnp.int32).at[target].set(cluster)
-    send_rank = jnp.zeros((slot_total,), jnp.int32).at[target].set(order_ranks)
-    slots = [
-        lax.all_to_all(a, "dp", split_axis=0, concat_axis=0, tiled=True) for a in (send_rows, send_cluster, send_rank)
-    ]
-    pieces = [lax.all_gather(a, "split", axis=0, tiled=True) for a in slots]
-    tile = 512
-    parts = []
-    for begin in range(0, slot_total, tile):
-        mine = [a[begin : begin + tile] for a in slots]
-        best = jnp.full((tile,), -1.0, jnp.float32)
-        for key in range(0, pieces[0].shape[0], tile):
-            best = jnp.maximum(best, pair_tile(*mine, *[a[key : key + tile] for a in pieces]))
-        parts.append(best)
-    returned = lax.all_to_all(jnp.concatenate(parts), "dp", split_axis=0, concat_axis=0, tiled=True)
-    return returned[target]
+    )(embeddings, cluster_ids, order_ranks)
 
 
 def shards(embeddings, cluster_ids, order_ranks):
-    nearest, flag = fast(embeddings, cluster_ids, order_ranks)
-    return lax.cond(
-        flag[0, 0] > 0,
-        lambda: padded(embeddings, cluster_ids, order_ranks),
-        lambda: nearest.reshape(ROWS),
-    )
+    args = (embeddings, cluster_ids.reshape(1, ROWS), order_ranks.reshape(1, ROWS))
+    nearest, flag = exchange(CAP, 0, *args)
+    nearest = lax.cond(flag[0, 0] > 0, lambda: exchange(FULL, 1, *args)[0], lambda: nearest)
+    return nearest.reshape(ROWS)
 
 
 def solution(mesh):

time: 93.8 us -> 81.2 us (0.87)
  between operations: 14 us -> 0.75 us
where the time goes in v2:
time: 81.2 us; the launch traced here: 81.1 us
  Pallas kernels  79.1 us (97%)
  local copies, waits for them, and re-layouts  1.23 us (2%)
    pallas_call x1, Pallas kernels, exchange(): pl.pallas_call(partial(kernel, cap), out_shape=(jax.ShapeDtypeStruct((1,...  79.1 us

profile of v2, /device:TPU:1, one launch (start us, length us, event | category | flops | bytes accessed | tf_op | source)
XLA Modules:
  0.0 81.1 jit_solution(7265192261462024363)
XLA Ops:
  0.0 0.0 copy-start
  0.0 79.1 %shard_map.39 = (f32[1,256]{1,0:T(1,128)S(1)}, s32[1,1]{1,0:T(1,128)}) custom-call(bf16[256,768]{1,0:T(8,128)(2,1)} %emb.1, s32[1,256]{1,0:T(1,128)} %bitcast.5, s32[1,256]{1,0:T(1,128)} %bitcast.7), custom_call_target="tpu_custom_call" | custom-call | tf_op jit(solution)/shard_map/pallas_call | solution.py:311
  79.1 0.0 copy-start.2
  79.8 0.0 copy-start.1
  79.8 0.0 copy-done
  79.8 0.0 copy-done.2
  79.8 0.7 copy-done.1
  80.5 0.6 copy.10
  (1 shorter events, 0.0 us)
Async XLA Ops:
  0.0 79.8 %copy-start = (bf16[256,768]{1,0:T(8,128)(2,1)S(1)}, bf16[256,768]{1,0:T(8,128)(2,1)}, u32[]{:S(2)}) copy-start(bf16[256,768]{1,0:T(8,128)(2,1)} %emb.1) | copy-start | bytes 1179652
  79.1 0.7 copy-start.2
  79.8 0.7 copy-start.1

commit v3 on v2

v3 whole, which is shorter than its diff:
```python
from functools import partial
import math

import jax
import jax.numpy as jnp
from jax import lax
from jax.experimental import pallas as pl
from jax.experimental.pallas import tpu as pltpu
from jax.sharding import PartitionSpec as P

MESH = pl.DeviceIdType.MESH

NX, NY, NZ = 4, 4, 16
CHIPS = NX * NY
ROWS = 256
WIDTH = 768
HALF = WIDTH // 2
MOST = 4
CAP = 32
FULL = MOST * CHIPS

STEPS = [0, 8, 4, 12, 7, 9, 1, 15, 6, 10, 2, 14, 3, 13, 5, 11]
COUNTS = [4, 4, 4, 2, 2]
GROUPS = len(COUNTS)
FIRST = [sum(COUNTS[:g]) for g in range(GROUPS)]
GROUP_OF = [g for g in range(GROUPS) for _ in range(COUNTS[g])]
SLOTS = [MOST * n for n in COUNTS]
XG = [CHIPS * n for n in SLOTS]
OFF = [sum(XG[:g]) for g in range(GROUPS)]
TOTAL = sum(XG)
WHOLE = 3
FAR_Z = sorted(range(1, NZ), key=lambda i: -min(STEPS[i], NZ - STEPS[i]))
FAR_E = sorted(range(1, CHIPS), key=lambda e: -(min(e // NY, NX - e // NY) + min(e % NY, NY - e % NY)))

BIG = 1 << 24
LATE = float(1 << 20)


def unit_rows(embeddings):
    values = embeddings.astype(jnp.float32)
    factor = lax.rsqrt(jnp.mean(values * values, axis=-1, keepdims=True) + 1e-06) * (
        1.0 / math.sqrt(values.shape[-1])
    )
    return (values * factor).astype(jnp.bfloat16)


def iota(shape, axis):
    return lax.broadcasted_iota(jnp.int32, shape, axis)


def one_hot(row, count):
    return jnp.where(iota((count, row.shape[1]), 0) == row, 1.0, 0.0)


def places(member):
    n = member.shape[1]
    before = jnp.where(iota((n, n), 0) < iota((n, n), 1), 1.0, 0.0).astype(jnp.bfloat16)
    counts = jnp.dot(member.astype(jnp.bfloat16), before, preferred_element_type=jnp.float32)
    return jnp.sum(member * counts, axis=0, keepdims=True).astype(jnp.int32)


def three_rows(a, b, c):
    sub = iota((8, a.shape[1]), 0)
    rows = jnp.where(sub == 0, a, jnp.where(sub == 1, b, jnp.where(sub == 2, c, 0.0)))
    return rows.astype(jnp.bfloat16)


def place_codes(codes, hot):
    parts = three_rows(
        (codes >> 16).astype(jnp.float32),
        ((codes >> 8) & 255).astype(jnp.float32),
        (codes & 255).astype(jnp.float32),
    )
    moved = lax.dot_general(parts, hot, (((1,), (1,)), ((), ())), preferred_element_type=jnp.float32)
    return (moved[0:1] * 65536.0 + moved[1:2] * 256.0 + moved[2:3]).astype(jnp.int32)


def fetch_values(values, hot):
    high = values.astype(jnp.bfloat16).astype(jnp.float32)
    rest = values - high
    middle = rest.astype(jnp.bfloat16).astype(jnp.float32)
    parts = three_rows(high, middle, rest - middle)
    moved = jnp.dot(parts, hot, preferred_element_type=jnp.float32)
    return (moved[0:1] + moved[1:2]) + moved[2:3]


def kernel(
    cap,
    emb_in, cluster_in, rank_in, out, flag,
    emb, cluster, rank, hot1, hot2, home, zsend, zrecv, xysend, half_out, half_in, own, other, key_rank,
    zmeta_out, zmeta_in, xymeta_out, xymeta_in, own_meta, other_meta,
    best_out, xyback, zback_out, zback,
    in_sem, zmeta_sem, zrow_send, zrow_recv, xymeta_sem, xyrow_send, xyrow_recv,
    cmeta_sem, crow_send, crow_recv, xyback_sem, zback_sem,
):
    dp, y = lax.axis_index("dp"), lax.axis_index("split")
    x, z, core = dp // (2 * NZ), (dp // 2) % NZ, dp % 2
    lanes = [n * cap for n in COUNTS]
    tiles = [max(1, n // 128) for n in lanes]
    tile0 = [sum(tiles[:g]) for g in range(GROUPS)]

    def along_z(step):
        return ((x * NZ + (z + step + NZ) % NZ) * 2 + core, y)

    def in_plane(e, sign):
        there_x = (x + sign * (e // NY) + NX) % NX
        there_y = (y + sign * (e % NY) + NY) % NY
        return ((there_x * NZ + z) * 2 + core, there_y)

    partner = (dp + 1 - 2 * core, y)

    barrier = pltpu.get_barrier_semaphore()
    for i in FAR_Z:
        pl.semaphore_signal(barrier, inc=1, device_id=along_z(STEPS[i]), device_id_type=MESH)
    for e in FAR_E:
        pl.semaphore_signal(barrier, inc=1, device_id=in_plane(e, 1), device_id_type=MESH)
    pl.semaphore_signal(barrier, inc=1, device_id=partner, device_id_type=MESH)
    loads = [
        pltpu.make_async_copy(src, dst, in_sem.at[n])
        for n, (src, dst) in enumerate(((cluster_in, cluster), (rank_in, rank), (emb_in, emb)))
    ]
    for load in loads:
        load.start()

    def send(src, dst, send_sem, recv_sem, device):
        pltpu.make_async_remote_copy(
            src_ref=src, dst_ref=dst, send_sem=send_sem, recv_sem=recv_sem, device_id=device, device_id_type=MESH
        ).start()

    def wait(ref, sem):
        pltpu.make_async_copy(ref, ref, sem).wait()

    loads[0].wait()
    loads[1].wait()
    ids = cluster[...]
    away = ((ids >> 4) - z) & (NZ - 1)
    step = jnp.zeros_like(ids)
    spot = jnp.zeros_like(ids)
    for i in range(NZ):
        g = GROUP_OF[i]
        step = jnp.where(away == STEPS[i], i, step)
        spot = jnp.where(away == STEPS[i], OFF[g] + MOST * (i - FIRST[g]), spot)
    place = places(one_hot(step, NZ))
    again = places(one_hot(ids, NZ * CHIPS))
    chip = ((((ids >> 2) & 3) - x) & 3) * NY + (((ids & 3) - y) & 3)
    spot = spot + again + chip * jnp.where(step < FIRST[WHOLE], SLOTS[0], SLOTS[WHOLE])
    slot = jnp.where(place < cap, step * cap + place, -1)
    most = jnp.max(place.astype(jnp.float32), axis=1, keepdims=True)
    codes = ((chip * MOST + again) << 17) + rank[...] + 1
    for g in range(GROUPS):
        rows = slice(FIRST[g] * cap, FIRST[g] * cap + lanes[g])
        hot = one_hot(slot - FIRST[g] * cap, lanes[g]).astype(jnp.bfloat16)
        hot1[rows, :] = hot
        placed = jnp.where(most >= cap, BIG, place_codes(codes, hot))
        width = min(128, lanes[g])
        for t in range(tiles[g]):
            zmeta_out[tile0[g] + t, :, 0:width] = placed[:, t * 128 : t * 128 + width]

    def code_row(i):
        g = GROUP_OF[i]
        return zmeta_out.at[tile0[g] + (i - FIRST[g]) * cap // 128]

    zmeta_in[0] = zmeta_out[0]
    loads[2].wait()
    unit = unit_rows(emb[...])
    for g in range(GROUPS):
        at = slice(FIRST[g] * cap, FIRST[g] * cap + lanes[g])
        rows = jnp.dot(hot1[at, :], unit, preferred_element_type=jnp.float32).astype(jnp.bfloat16)
        zsend[at, :] = rows
        if g == 0:
            zrecv[0:cap, :] = rows[0:cap]
            pl.semaphore_wait(barrier, NZ - 1 + CHIPS - 1 + 1)
            for i in FAR_Z:
                send(code_row(i), zmeta_in.at[i], zmeta_sem.at[0], zmeta_sem.at[1], along_z(STEPS[i]))
        for i in range(max(1, FIRST[g]), FIRST[g] + COUNTS[g]):
            span = pl.ds(i * cap, cap)
            send(zsend.at[span], zrecv.at[span], zrow_send.at[0], zrow_recv.at[g], along_z(STEPS[i]))
    home[...] = one_hot(spot, TOTAL).astype(jnp.bfloat16)

    wait(zmeta_in.at[pl.ds(1, NZ - 1)], zmeta_sem.at[1])
    sub8 = iota((8, 128), 0)
    lane8 = iota((8, 128), 1)
    over = jnp.zeros((1, 1), jnp.float32)
    meta = [jnp.zeros((8, 128), jnp.int32), jnp.zeros((8, 128), jnp.int32)]
    for g in range(GROUPS):
        width = min(128, lanes[g])
        parts = []
        for t in range(tiles[g]):
            first = FIRST[g] + t * 128 // cap
            row = zmeta_in[first, :, 0:width]
            for q in range(1, width // cap):
                row = jnp.where(iota((1, width), 1) // cap == q, zmeta_in[first + q, :, 0:width], row)
            parts.append(row)
        codes = parts[0] if tiles[g] == 1 else jnp.concatenate(parts, axis=1)
        over = jnp.maximum(over, jnp.max(codes.astype(jnp.float32), axis=1, keepdims=True))
        filled = (codes > 0) & (codes < BIG)
        value = codes - 1
        source = iota((1, lanes[g]), 1) // cap
        target = (value >> 19) * SLOTS[g] + source * MOST + ((value >> 17) & 3)
        hot = one_hot(jnp.where(filled, target, -1), XG[g]).astype(jnp.bfloat16)
        hot2[OFF[g] : OFF[g] + XG[g], 0 : lanes[g]] = hot
        ranks = place_codes(jnp.where(filled, (value & 131071) + 1, 0), hot)
        for h in range(2):
            part = ranks[:, h * 128 : (h + 1) * 128] if g < WHOLE else ranks
            meta[h] = jnp.where(sub8 == g, part, meta[h])
    for h in range(2):
        xymeta_out[h] = jnp.where(over >= BIG, BIG, meta[h])
    xymeta_in[0] = xymeta_out[0]
    for e in FAR_E:
        send(xymeta_out.at[e // 8], xymeta_in.at[e], xymeta_sem.at[0], xymeta_sem.at[1], in_plane(e, 1))

    def from_chips(ref):
        out = []
        for h in range(2):
            tile = ref[h * 8]
            for e in range(h * 8 + 1, h * 8 + 8):
                owned = ((sub8 < WHOLE) & (lane8 // 16 == e % 8)) | ((sub8 >= WHOLE) & (lane8 // 8 == e))
                tile = jnp.where(owned, ref[e], tile)
            out.append(tile)
        joined = jnp.where(lane8 < 64, out[0], out[1])
        return [jnp.where(sub8 < WHOLE, tile, joined) for tile in out]

    def parts_of(g):
        return 2 if g < WHOLE else 1

    def plane_ranks():
        wait(xymeta_in.at[pl.ds(1, CHIPS - 1)], xymeta_sem.at[1])
        merged = from_chips(xymeta_in)
        for h in range(2):
            own_meta[h] = merged[h]
        send(own_meta, other_meta, cmeta_sem.at[0], cmeta_sem.at[1], partner)

        rows = [[merged[h][g : g + 1].astype(jnp.float32) for h in range(parts_of(g))] for g in range(GROUPS)]
        wait(other_meta, cmeta_sem.at[1])
        top = jnp.zeros((8, 128), jnp.float32)
        for which, ref in enumerate((own_meta, other_meta)):
            for h in range(2):
                tile = ref[h].astype(jnp.float32)
                top = jnp.maximum(top, tile)
                for g in range(GROUPS):
                    if h < parts_of(g):
                        row = tile[g : g + 1]
                        key = jnp.where(row > 0.0, row, LATE)
                        at = which * TOTAL + OFF[g] + h * 128
                        key_rank[at : at + 128, :] = jnp.transpose(jnp.broadcast_to(key, (128, 128)))
        flag[...] = jnp.where(jnp.max(top, axis=(0, 1), keepdims=True) >= BIG, 1, 0)
        return rows

    best = [[jnp.full((1, 128), -1.0, jnp.float32) for _ in range(parts_of(g))] for g in range(GROUPS)]

    def score(which, first, last, g0, g1):
        k0, k1 = OFF[first], OFF[last - 1] + XG[last - 1]
        q0, q1 = OFF[g0], OFF[g1 - 1] + XG[g1 - 1]
        scores = lax.dot_general(
            (own, other)[which][k0:k1, :], own[q0:q1, :], (((1,), (1,)), ((), ())), preferred_element_type=jnp.float32
        )
        ranks = key_rank[which * TOTAL + k0 : which * TOTAL + k1, :]
        for g in range(g0, g1):
            for h in range(parts_of(g)):
                at = OFF[g] - q0 + h * 128
                part = jnp.where(ranks < query_rank[g][h], scores[:, at : at + 128], -1.0)
                best[g][h] = jnp.maximum(best[g][h], jnp.max(part, axis=0, keepdims=True))

    def score_group(which, g):
        score(which, 0, g + 1, g, g + 1)
        if g:
            score(which, g, g + 1, 0, g)

    def group_in_plane(g):
        first, end = max(1, FIRST[g]) * cap, FIRST[g] * cap + lanes[g]
        wait(zrecv.at[pl.ds(first, end - first)], zrow_recv.at[g])
        rows = jnp.dot(
            hot2[OFF[g] : OFF[g] + XG[g], 0 : lanes[g]],
            zrecv[FIRST[g] * cap : end, :],
            preferred_element_type=jnp.float32,
        )
        if g < WHOLE:
            rows = rows.astype(jnp.bfloat16)
            xysend[OFF[g] : OFF[g] + XG[g], :] = rows
            own[OFF[g] : OFF[g] + 16, :] = rows[0:16]
            src, dst, base = xysend, own, OFF[g]
        else:
            rows = rows.reshape(CHIPS, 8, WIDTH)
            rows = jnp.concatenate([rows[:, :, :HALF], rows[:, :, HALF:]], axis=1).reshape(CHIPS * 16, HALF)
            rows = rows.astype(jnp.bfloat16)
            src, dst, base = half_out, half_in, (g - WHOLE) * CHIPS * 16
            half_out[base : base + CHIPS * 16, :] = rows
            half_in[base : base + 16, :] = rows[0:16]
        for e in FAR_E:
            span = pl.ds(base + e * 16, 16)
            send(src.at[span], dst.at[span], xyrow_send.at[g], xyrow_recv.at[g], in_plane(e, 1))

    def wait_plane(g, sem):
        ref, base = (own, OFF[g]) if g < WHOLE else (half_in, (g - WHOLE) * CHIPS * 16)
        wait(ref.at[pl.ds(base + 16, CHIPS * 16 - 16)], sem)

    def group_to_partner(g):
        wait_plane(g, xyrow_recv.at[g])
        if g >= WHOLE:
            base = (g - WHOLE) * CHIPS * 16
            rows = half_in[base : base + CHIPS * 16, :].astype(jnp.float32).reshape(CHIPS, 16, HALF)
            rows = jnp.concatenate([rows[:, :8], rows[:, 8:]], axis=2).reshape(CHIPS * 8, WIDTH)
            own[OFF[g] : OFF[g] + XG[g], :] = rows.astype(jnp.bfloat16)
        span = pl.ds(OFF[g], XG[g])
        send(own.at[span], other.at[span], crow_send.at[0], crow_recv.at[g], partner)

    def group_from_partner(g):
        wait(other.at[pl.ds(OFF[g], XG[g])], crow_recv.at[g])

    for g in range(GROUPS):
        group_in_plane(g)
        if g == 0:
            query_rank = plane_ranks()
        if g >= 1:
            group_to_partner(g - 1)
        if g >= 2:
            group_from_partner(g - 2)
            for which in range(2):
                score_group(which, g - 2)
    group_from_partner(GROUPS - 2)
    for which in range(2):
        score_group(which, GROUPS - 2)
    group_to_partner(GROUPS - 1)
    score_group(0, GROUPS - 1)
    group_from_partner(GROUPS - 1)
    score_group(1, GROUPS - 1)

    for h in range(2):
        tile = jnp.zeros((8, 128), jnp.float32)
        for g in range(GROUPS):
            tile = jnp.where(sub8 == g, best[g][h if g < WHOLE else 0], tile)
        best_out[h] = tile
    xyback[0] = best_out[0]
    for e in FAR_E:
        send(best_out.at[e // 8], xyback.at[e], xyback_sem.at[0], xyback_sem.at[1], in_plane(e, -1))
    wait(xyback.at[pl.ds(1, CHIPS - 1)], xyback_sem.at[1])
    merged = from_chips(xyback)
    for g in range(GROUPS):
        for h in range(2):
            zback_out[g, h : h + 1, :] = merged[h][g : g + 1]
    zback[0] = zback_out[0]
    for i in FAR_Z:
        send(zback_out.at[GROUP_OF[i]], zback.at[i], zback_sem.at[0], zback_sem.at[1], along_z(-STEPS[i]))
    wait(zback.at[pl.ds(1, NZ - 1)], zback_sem.at[1])
    parts = []
    lane2 = iota((2, 128), 1)
    for g in range(GROUPS):
        row = zback[FIRST[g]]
        for q in range(1, COUNTS[g]):
            row = jnp.where((lane2 // MOST) % COUNTS[g] == q, zback[FIRST[g] + q], row)
        parts += [row[h : h + 1] for h in range(parts_of(g))]
    out[...] = fetch_values(jnp.concatenate(parts, axis=1), home[...])

    wait(zmeta_in.at[pl.ds(1, NZ - 1)], zmeta_sem.at[0])
    wait(zsend.at[pl.ds(cap, (NZ - 1) * cap)], zrow_send.at[0])
    wait(xymeta_in.at[pl.ds(1, CHIPS - 1)], xymeta_sem.at[0])
    for g in range(GROUPS):
        wait_plane(g, xyrow_send.at[g])
    wait(own_meta, cmeta_sem.at[0])
    wait(own, crow_send.at[0])
    wait(xyback.at[pl.ds(1, CHIPS - 1)], xyback_sem.at[0])
    wait(zback.at[pl.ds(1, NZ - 1)], zback_sem.at[0])


def exchange(cap, collective_id, embeddings, cluster_ids, order_ranks):
    vmem = pl.BlockSpec(memory_space=pltpu.VMEM)
    anywhere = pl.BlockSpec(memory_space=pl.ANY)
    bf16, f32, i32 = jnp.bfloat16, jnp.float32, jnp.int32
    rows_of_codes = sum(max(1, n * cap // 128) for n in COUNTS)

    def sems(n):
        return pltpu.SemaphoreType.DMA((n,))

    return pl.pallas_call(
        partial(kernel, cap),
        out_shape=(jax.ShapeDtypeStruct((1, ROWS), f32), jax.ShapeDtypeStruct((1, 1), i32)),
        in_specs=[anywhere] * 3,
        out_specs=(vmem, vmem),
        scratch_shapes=[
            pltpu.VMEM((ROWS, WIDTH), bf16),
            pltpu.VMEM((1, ROWS), i32),
            pltpu.VMEM((1, ROWS), i32),
            pltpu.VMEM((NZ * cap, ROWS), bf16),
            pltpu.VMEM((TOTAL, MOST * cap), bf16),
            pltpu.VMEM((TOTAL, ROWS), bf16),
            pltpu.VMEM((NZ * cap, WIDTH), bf16),
            pltpu.VMEM((NZ * cap, WIDTH), bf16),
            pltpu.VMEM((OFF[WHOLE], WIDTH), bf16),
            pltpu.VMEM(((GROUPS - WHOLE) * CHIPS * 16, HALF), bf16),
            pltpu.VMEM(((GROUPS - WHOLE) * CHIPS * 16, HALF), bf16),
            pltpu.VMEM((TOTAL, WIDTH), bf16),
            pltpu.VMEM((TOTAL, WIDTH), bf16),
            pltpu.VMEM((2 * TOTAL, 128), f32),
            pltpu.VMEM((rows_of_codes, 1, 128), i32),
            pltpu.VMEM((NZ, 1, 128), i32),
            pltpu.VMEM((2, 8, 128), i32),
            pltpu.VMEM((CHIPS, 8, 128), i32),
            pltpu.VMEM((2, 8, 128), i32),
            pltpu.VMEM((2, 8, 128), i32),
            pltpu.VMEM((2, 8, 128), f32),
            pltpu.VMEM((CHIPS, 8, 128), f32),
            pltpu.VMEM((GROUPS, 2, 128), f32),
            pltpu.VMEM((NZ, 2, 128), f32),
            sems(3), sems(2), sems(1), sems(GROUPS), sems(2), sems(GROUPS), sems(GROUPS),
            sems(2), sems(1), sems(GROUPS), sems(2), sems(2),
        ],
        compiler_params=pltpu.CompilerParams(
            collective_id=collective_id, has_side_effects=True, vmem_limit_bytes=40 * 1024 * 1024
        ),
    )(embeddings, cluster_ids, order_ranks)


def shards(embeddings, cluster_ids, order_ranks):
    args = (embeddings, cluster_ids.reshape(1, ROWS), order_ranks.reshape(1, ROWS))
    nearest, flag = exchange(CAP, 0, *args)
    nearest = lax.cond(flag[0, 0] > 0, lambda: exchange(FULL, 1, *args)[0], lambda: nearest)
    return nearest.reshape(ROWS)


def solution(mesh):
    in_specs = (P(("dp", "split"), None), P(("dp", "split"), None), P(("dp", "split")))
    out_specs = P(("dp", "split"))
    return jax.shard_map(shards, mesh=mesh, in_specs=in_specs, out_specs=out_specs, check_vma=False)
```

time: 81.2 us -> 76.4 us (0.941)
  Pallas kernels: 79.1 us -> 74.2 us
    pallas_call x1, Pallas kernels: 79.1 us -> 74.2 us  [exchange(): pl.pallas_call(partial(kernel, cap), out_shape=(jax.ShapeDtypeStruct((1,...]
where the time goes in v3:
time: 76.4 us; the launch traced here: 76.2 us
  Pallas kernels  74.2 us (97%)
  local copies, waits for them, and re-layouts  1.23 us (2%)
    pallas_call x1, Pallas kernels, exchange(): pl.pallas_call(partial(kernel, cap), out_shape=(jax.ShapeDtypeStruct((1,...  74.2 us

profile of v3, /device:TPU:1, one launch (start us, length us, event | category | flops | bytes accessed | tf_op | source)
XLA Modules:
  0.0 76.2 jit_solution(5675926880493764761)
XLA Ops:
  0.0 0.0 copy-start
  0.0 74.2 %shard_map.39 = (f32[1,256]{1,0:T(1,128)S(1)}, s32[1,1]{1,0:T(1,128)}) custom-call(bf16[256,768]{1,0:T(8,128)(2,1)} %emb_in.1, s32[1,256]{1,0:T(1,128)} %bitcast.5, s32[1,256]{1,0:T(1,128)} %bitcast.7), custom_call_target="tpu_custom_call" | custom-call | tf_op jit(solution)/shard_map/pallas_call | solution.py:374
  74.2 0.0 copy-start.2
  75.0 0.0 copy-start.1
  75.0 0.0 copy-done
  75.0 0.0 copy-done.2
  75.0 0.7 copy-done.1
  75.6 0.6 copy.10
  (1 shorter events, 0.0 us)
Async XLA Ops:
  0.0 75.0 %copy-start = (bf16[256,768]{1,0:T(8,128)(2,1)S(1)}, bf16[256,768]{1,0:T(8,128)(2,1)}, u32[]{:S(2)}) copy-start(bf16[256,768]{1,0:T(8,128)(2,1)} %emb_in.1) | copy-start | bytes 1179652
  74.2 0.7 copy-start.2
  75.0 0.7 copy-start.1

commit v4 on v3

--- a/solution.py
+++ b/solution.py
@@ -32,6 +32,12 @@
 FAR_Z = sorted(range(1, NZ), key=lambda i: -min(STEPS[i], NZ - STEPS[i]))
 FAR_E = sorted(range(1, CHIPS), key=lambda e: -(min(e // NY, NX - e // NY) + min(e % NY, NY - e % NY)))
 
+RELAY = NZ // 4
+NEAR_Z = [i for i in FAR_Z if min(STEPS[i], NZ - STEPS[i]) <= RELAY]
+BEYOND_Z = [i for i in FAR_Z if i not in NEAR_Z]
+SEND_NEAR = [4, 12]
+SEND = [8, 7, 9, 1, 15, 6, 10, 2, 14, 3, 13, 5, 11]
+
 BIG = 1 << 24
 LATE = float(1 << 20)
 
@@ -87,10 +93,10 @@
 def kernel(
     cap,
     emb_in, cluster_in, rank_in, out, flag,
-    emb, cluster, rank, hot1, hot2, home, zsend, zrecv, xysend, half_out, half_in, own, other, key_rank,
+    emb, cluster, rank, hot1, hot2, home, zsend, zrecv, xysend, half_out, half_in, half_other, own, other, key_rank,
     zmeta_out, zmeta_in, xymeta_out, xymeta_in, own_meta, other_meta,
     best_out, xyback, zback_out, zback,
-    in_sem, zmeta_sem, zrow_send, zrow_recv, xymeta_sem, xyrow_send, xyrow_recv,
+    beyond, in_sem, zmeta_sem, zrow_send, zrow_recv, xymeta_sem, xyrow_send, xyrow_recv,
     cmeta_sem, crow_send, crow_recv, xyback_sem, zback_sem,
 ):
     dp, y = lax.axis_index("dp"), lax.axis_index("split")
@@ -110,7 +116,7 @@
     partner = (dp + 1 - 2 * core, y)
 
     barrier = pltpu.get_barrier_semaphore()
-    for i in FAR_Z:
+    for i in NEAR_Z:
         pl.semaphore_signal(barrier, inc=1, device_id=along_z(STEPS[i]), device_id_type=MESH)
     for e in FAR_E:
         pl.semaphore_signal(barrier, inc=1, device_id=in_plane(e, 1), device_id_type=MESH)
@@ -169,12 +175,26 @@
         zsend[at, :] = rows
         if g == 0:
             zrecv[0:cap, :] = rows[0:cap]
-            pl.semaphore_wait(barrier, NZ - 1 + CHIPS - 1 + 1)
-            for i in FAR_Z:
-                send(code_row(i), zmeta_in.at[i], zmeta_sem.at[0], zmeta_sem.at[1], along_z(STEPS[i]))
-        for i in range(max(1, FIRST[g]), FIRST[g] + COUNTS[g]):
-            span = pl.ds(i * cap, cap)
-            send(zsend.at[span], zrecv.at[span], zrow_send.at[0], zrow_recv.at[g], along_z(STEPS[i]))
+
+    def send_rows(i):
+        span = pl.ds(i * cap, cap)
+        send(zsend.at[span], zrecv.at[span], zrow_send.at[0], zrow_recv.at[GROUP_OF[i]], along_z(STEPS[i]))
+
+    def send_codes(i):
+        send(code_row(i), zmeta_in.at[i], zmeta_sem.at[0], zmeta_sem.at[1], along_z(STEPS[i]))
+
+    pl.semaphore_wait(barrier, len(NEAR_Z) + CHIPS - 1 + 1)
+    for to in (RELAY, -RELAY):
+        pl.semaphore_signal(beyond, inc=1, device_id=along_z(to), device_id_type=MESH)
+    for i in NEAR_Z:
+        send_codes(i)
+    for d in SEND_NEAR:
+        send_rows(STEPS.index(d))
+    pl.semaphore_wait(beyond, 2)
+    for i in BEYOND_Z:
+        send_codes(i)
+    for d in SEND:
+        send_rows(STEPS.index(d))
     home[...] = one_hot(spot, TOTAL).astype(jnp.bfloat16)
 
     wait(zmeta_in.at[pl.ds(1, NZ - 1)], zmeta_sem.at[1])
@@ -261,10 +281,14 @@
                 part = jnp.where(ranks < query_rank[g][h], scores[:, at : at + 128], -1.0)
                 best[g][h] = jnp.maximum(best[g][h], jnp.max(part, axis=0, keepdims=True))
 
-    def score_group(which, g):
-        score(which, 0, g + 1, g, g + 1)
+    def score_own(g):
+        score(0, 0, g + 1, g, g + 1)
         if g:
-            score(which, g, g + 1, 0, g)
+            score(1, 0, g, g, g + 1)
+            score(0, g, g + 1, 0, g)
+
+    def score_other(g):
+        score(1, g, g + 1, 0, g + 1)
 
     def group_in_plane(g):
         first, end = max(1, FIRST[g]) * cap, FIRST[g] * cap + lanes[g]
@@ -294,18 +318,29 @@
         ref, base = (own, OFF[g]) if g < WHOLE else (half_in, (g - WHOLE) * CHIPS * 16)
         wait(ref.at[pl.ds(base + 16, CHIPS * 16 - 16)], sem)
 
+    def to_partner(g):
+        if g < WHOLE:
+            return own, other, pl.ds(OFF[g], XG[g])
+        return half_in, half_other, pl.ds((g - WHOLE) * CHIPS * 16, CHIPS * 16)
+
+    def full_width(ref, g):
+        base = (g - WHOLE) * CHIPS * 16
+        rows = ref[base : base + CHIPS * 16, :].astype(jnp.float32).reshape(CHIPS, 16, HALF)
+        rows = jnp.concatenate([rows[:, :8], rows[:, 8:]], axis=2).reshape(CHIPS * 8, WIDTH)
+        return rows.astype(jnp.bfloat16)
+
     def group_to_partner(g):
         wait_plane(g, xyrow_recv.at[g])
+        src, dst, span = to_partner(g)
+        send(src.at[span], dst.at[span], crow_send.at[g], crow_recv.at[g], partner)
         if g >= WHOLE:
-            base = (g - WHOLE) * CHIPS * 16
-            rows = half_in[base : base + CHIPS * 16, :].astype(jnp.float32).reshape(CHIPS, 16, HALF)
-            rows = jnp.concatenate([rows[:, :8], rows[:, 8:]], axis=2).reshape(CHIPS * 8, WIDTH)
-            own[OFF[g] : OFF[g] + XG[g], :] = rows.astype(jnp.bfloat16)
-        span = pl.ds(OFF[g], XG[g])
-        send(own.at[span], other.at[span], crow_send.at[0], crow_recv.at[g], partner)
+            own[OFF[g] : OFF[g] + XG[g], :] = full_width(half_in, g)
 
     def group_from_partner(g):
-        wait(other.at[pl.ds(OFF[g], XG[g])], crow_recv.at[g])
+        _, dst, span = to_partner(g)
+        wait(dst.at[span], crow_recv.at[g])
+        if g >= WHOLE:
+            other[OFF[g] : OFF[g] + XG[g], :] = full_width(half_other, g)
 
     for g in range(GROUPS):
         group_in_plane(g)
@@ -314,16 +349,16 @@
         if g >= 1:
             group_to_partner(g - 1)
         if g >= 2:
+            score_own(g - 2)
             group_from_partner(g - 2)
-            for which in range(2):
-                score_group(which, g - 2)
+            score_other(g - 2)
+    score_own(GROUPS - 2)
     group_from_partner(GROUPS - 2)
-    for which in range(2):
-        score_group(which, GROUPS - 2)
+    score_other(GROUPS - 2)
     group_to_partner(GROUPS - 1)
-    score_group(0, GROUPS - 1)
+    score_own(GROUPS - 1)
     group_from_partner(GROUPS - 1)
-    score_group(1, GROUPS - 1)
+    score_other(GROUPS - 1)
 
     for h in range(2):
         tile = jnp.zeros((8, 128), jnp.float32)
@@ -357,7 +392,9 @@
     for g in range(GROUPS):
         wait_plane(g, xyrow_send.at[g])
     wait(own_meta, cmeta_sem.at[0])
-    wait(own, crow_send.at[0])
+    for g in range(GROUPS):
+        _, dst, span = to_partner(g)
+        wait(dst.at[span], crow_send.at[g])
     wait(xyback.at[pl.ds(1, CHIPS - 1)], xyback_sem.at[0])
     wait(zback.at[pl.ds(1, NZ - 1)], zback_sem.at[0])
 
@@ -388,6 +425,7 @@
             pltpu.VMEM((OFF[WHOLE], WIDTH), bf16),
             pltpu.VMEM(((GROUPS - WHOLE) * CHIPS * 16, HALF), bf16),
             pltpu.VMEM(((GROUPS - WHOLE) * CHIPS * 16, HALF), bf16),
+            pltpu.VMEM(((GROUPS - WHOLE) * CHIPS * 16, HALF), bf16),
             pltpu.VMEM((TOTAL, WIDTH), bf16),
             pltpu.VMEM((TOTAL, WIDTH), bf16),
             pltpu.VMEM((2 * TOTAL, 128), f32),
@@ -401,11 +439,11 @@
             pltpu.VMEM((CHIPS, 8, 128), f32),
             pltpu.VMEM((GROUPS, 2, 128), f32),
             pltpu.VMEM((NZ, 2, 128), f32),
-            sems(3), sems(2), sems(1), sems(GROUPS), sems(2), sems(GROUPS), sems(GROUPS),
-            sems(2), sems(1), sems(GROUPS), sems(2), sems(2),
+            pltpu.SemaphoreType.REGULAR, sems(3), sems(2), sems(1), sems(GROUPS), sems(2), sems(GROUPS), sems(GROUPS),
+            sems(2), sems(GROUPS), sems(GROUPS), sems(2), sems(2),
         ],
         compiler_params=pltpu.CompilerParams(
-            collective_id=collective_id, has_side_effects=True, vmem_limit_bytes=40 * 1024 * 1024
+            collective_id=collective_id, has_side_effects=True, vmem_limit_bytes=60 * 1024 * 1024
         ),
     )(embeddings, cluster_ids, order_ranks)
 

time: 76.4 us -> 74.4 us (0.974)
  Pallas kernels: 74.2 us -> 72.2 us
    pallas_call x1, Pallas kernels: 74.2 us -> 72.2 us  [exchange(): pl.pallas_call(partial(kernel, cap), out_shape=(jax.ShapeDtypeStruct((1,...]
where the time goes in v4:
time: 74.4 us; the launch traced here: 74.2 us
  Pallas kernels  72.2 us (97%)
  local copies, waits for them, and re-layouts  1.23 us (2%)
  between operations  0.75 us (1%)
    pallas_call x1, Pallas kernels, exchange(): pl.pallas_call(partial(kernel, cap), out_shape=(jax.ShapeDtypeStruct((1,...  72.2 us

profile of v4, /device:TPU:1, one launch (start us, length us, event | category | flops | bytes accessed | tf_op | source)
XLA Modules:
  0.0 74.2 jit_solution(9796315466302236056)
XLA Ops:
  0.0 0.0 copy-start
  0.0 72.2 %shard_map.39 = (f32[1,256]{1,0:T(1,128)S(1)}, s32[1,1]{1,0:T(1,128)}) custom-call(bf16[256,768]{1,0:T(8,128)(2,1)} %emb_in.1, s32[1,256]{1,0:T(1,128)} %bitcast.5, s32[1,256]{1,0:T(1,128)} %bitcast.7), custom_call_target="tpu_custom_call" | custom-call | tf_op jit(solution)/shard_map/pallas_call | solution.py:411
  72.3 0.0 copy-start.2
  73.0 0.0 copy-start.1
  73.0 0.0 copy-done
  73.0 0.0 copy-done.2
  73.0 0.7 copy-done.1
  73.7 0.6 copy.10
  (1 shorter events, 0.0 us)
Async XLA Ops:
  0.0 73.0 %copy-start = (bf16[256,768]{1,0:T(8,128)(2,1)S(1)}, bf16[256,768]{1,0:T(8,128)(2,1)}, u32[]{:S(2)}) copy-start(bf16[256,768]{1,0:T(8,128)(2,1)} %emb_in.1) | copy-start | bytes 1179652
  72.3 0.7 copy-start.2
  73.0 0.7 copy-start.1
